TPU v7x, 512 devices: a whole 4x8x8 slice. The times are simulated.
512 devices in a mesh: frame: 64 (over z, y_hi, core), head: 8 (over x, y_lo).
Axes of the slice: x: 4, y: 8 (y_hi: 4, y_lo: 2; y = y_hi * 2 + y_lo), z: 8, core: 2. Of those that a mesh axis runs over, the one named last changes fastest.
Arguments:
- q_high: bfloat16 [12288, 5120], P('frame', 'head'), may hold values from -32 to 32, as said below
- k_high: bfloat16 [12288, 5120], P('frame', 'head'), may hold values from -32 to 32
- v_high: bfloat16 [12288, 5120], P('frame', 'head'), may hold values from -6 to 6
- gain_qh: float32 [5120], P('head'), may hold values from 0.5 to 2
- gain_kh: float32 [5120], P('head'), may hold values from 0.5 to 2
- q_low: bfloat16 [12288, 5120], P(('frame', 'head')), may hold values from -32 to 32
- k_low: bfloat16 [12288, 5120], P(('frame', 'head')), may hold values from -32 to 32
- v_low: bfloat16 [12288, 5120], P(('frame', 'head')), may hold values from -6 to 6
- gain_ql: float32 [5120], replicated, may hold values from 0.5 to 2
- gain_kl: float32 [5120], replicated, may hold values from 0.5 to 2
- keyframes: int32 [2], replicated, may hold values from 0 to 63
- switch_step: int32 [1], replicated, may hold values from 10 to 30
- permutation: int32 [192], replicated, may hold values from 0 to 191, each once
Outputs:
- blended: bfloat16 [12288, 5120], P(('frame', 'head'))
Inputs may be any that keep to these rules, and one draw needn't show every extreme that they name: `q_high`: each row of the query and key arrays is of order one in mean square over all channels.
All inputs are finite; a program needn't handle non-finite values.
Results may differ from a plain program's by a relative error of at most 0.012.
Values may be sent and summed in bfloat16 or wider, within the bound.
A program may use at most 64 MiB of HBM per device.

v0:
```python
import jax
import jax.numpy as jnp
from jax import lax
from jax.sharding import PartitionSpec as P

HEADS = 40
HD = 128
STEPS = 40


epsilon = 1e-06


def spread(block, axis, holder):
    block = jnp.where(lax.axis_index(axis) == holder, block, jnp.zeros_like(block))
    return lax.psum(block, axis)


def attend(query, keys, values, head_size):
    rows = query.shape[0]
    groups = query.shape[1] // head_size
    qheads = query.reshape(rows, groups, head_size).transpose(1, 0, 2)
    kheads = keys.reshape(keys.shape[0], groups, head_size).transpose(1, 0, 2)
    vheads = values.reshape(values.shape[0], groups, head_size).transpose(1, 0, 2)

    def one_head(items):
        qpart, kpart, vpart = items
        scores = jnp.einsum(
            "qd,kd->qk", qpart, kpart, preferred_element_type=jnp.float32
        ) * head_size ** (-0.5)
        top = jnp.max(scores, axis=-1, keepdims=True)
        expo = jnp.exp(scores - top)
        weights = (expo / jnp.sum(expo, axis=-1, keepdims=True)).astype(jnp.bfloat16)
        return jnp.einsum("qk,kd->qd", weights, vpart, preferred_element_type=jnp.float32).astype(
            jnp.bfloat16
        )

    outputs = lax.map(one_head, (qheads, kheads, vheads))
    return outputs.transpose(1, 0, 2).reshape(rows, groups * head_size)


def scaled(values, mean_square, gain):
    factor = lax.rsqrt(mean_square + epsilon)[:, None]
    return (values.astype(jnp.float32) * factor * gain).astype(jnp.bfloat16)


def squares(values):
    floats = values.astype(jnp.float32)
    return jnp.sum(floats * floats, axis=1)


def body(
    q_high,
    k_high,
    v_high,
    gain_qh,
    gain_kh,
    q_low,
    k_low,
    v_low,
    gain_ql,
    gain_kl,
    keyframes,
    switch_step,
    permutation,
):
    width = HEADS * HD
    count = keyframes.shape[0]
    sum_q, sum_k = lax.psum((squares(q_high), squares(k_high)), "head")
    qn_high = scaled(q_high, sum_q / width, gain_qh)
    kn_high = scaled(k_high, sum_k / width, gain_kh)
    qn_low = scaled(q_low, squares(q_low) / width, gain_ql)
    kn_low = scaled(k_low, squares(k_low) / width, gain_kl)
    heads_q, heads_k, heads_v = (
        lax.all_to_all(qn_low, "head", split_axis=1, concat_axis=0, tiled=True),
        lax.all_to_all(kn_low, "head", split_axis=1, concat_axis=0, tiled=True),
        lax.all_to_all(v_low, "head", split_axis=1, concat_axis=0, tiled=True),
    )
    high_keys = [kn_high]
    high_vals = [v_high]
    low_keys = [heads_k]
    low_vals = [heads_v]
    for index in range(count):
        got_k, got_v = (
            spread(kn_high, "frame", keyframes[index]),
            spread(v_high, "frame", keyframes[index]),
        )
        high_keys.append(got_k)
        high_vals.append(got_v)
    for index in range(count):
        got_k, got_v = (
            spread(heads_k, "frame", keyframes[index]),
            spread(heads_v, "frame", keyframes[index]),
        )
        low_keys.append(got_k)
        low_vals.append(got_v)
    o_high = attend(
        qn_high, jnp.concatenate(high_keys, axis=0), jnp.concatenate(high_vals, axis=0), HD
    )
    o_low = attend(
        heads_q, jnp.concatenate(low_keys, axis=0), jnp.concatenate(low_vals, axis=0), HD
    )
    moved = jnp.take(o_high, permutation, axis=0)
    lam = switch_step[0].astype(jnp.float32) / STEPS
    mixed = ((1.0 - lam) * moved.astype(jnp.float32) + lam * o_low.astype(jnp.float32)).astype(
        jnp.bfloat16
    )
    return lax.all_to_all(mixed, "head", split_axis=0, concat_axis=1, tiled=True)


def solution(mesh):
    return jax.shard_map(
        body,
        mesh=mesh,
        in_specs=(
            P("frame", "head"),
            P("frame", "head"),
            P("frame", "head"),
            P("head"),
            P("head"),
            P(("frame", "head"), None),
            P(("frame", "head"), None),
            P(("frame", "head"), None),
            P(),
            P(),
            P(),
            P(),
            P(),
        ),
        out_specs=P(("frame", "head"), None),
        check_vma=False,
    )
```

profile of v0, /device:TPU:1, one launch (start us, length us, event | category | flops | bytes accessed | tf_op | source)
XLA Modules:
  0.0 665.7 jit_solution(9089298241696324549)
XLA Ops:
  6.5 1.2 fusion.31
  7.7 1.1 fusion.33
  9.6 5.9 all-to-all-start.1
  15.7 16.8 %all-reduce = (f32[192]{0:T(256)S(1)}, f32[192]{0:T(256)S(1)}) all-reduce(f32[192]{0:T(256)S(1)} %fusion.22, f32[192]{0:T(256)S(1)} %fusion.25), channel_id=1, replica_groups=mesh['frame'=64,'head'=8] {'head'}, use_global_device_ids=true, to_apply=%region_1.0 | all-reduce | flops 384 | bytes 3072 | tf_op jit(solution)/shard_map/psum | solution.py:69
  35.3 1.1 broadcast_select_fusion.6
  36.4 3.4 all-to-all-start.2
  40.5 5.2 all-to-all-done.2
  51.6 3.4 all-to-all-start
  57.6 3.4 all-to-all-done
  62.0 561.0 %all-reduce.4.cloned.1.call-done = (bf16[192,5,128]{2,1,0:T(8,128)(2,1)}, bf16[192,5,128]{2,1,0:T(8,128)(2,1)}, bf16[192,5,128]{2,1,0:T(8,128)(2,1)}, bf16[192,5...) async-done(((bf16[192,5,128]{2,1,0:T(8,128)(2,1)}, ...) | async-done | bytes 1966096 | tf_op jit(solution)/shard_map/psum | solution.py:16
  623.1 1.1 pad_maximum_fusion
  626.5 8.6 %while.20 = (s32[]{:T(128)}, bf16[5,192,128]{2,1,0:T(8,128)(2,1)S(1)}, bf16[5,192,128]{2,1,0:T(8,128)(2,1)}, bf16[5,576,128]{2,1,0:T(8,128)(2,1)S(1)}, bf16[5,576,128]{2,1,0:T(8,128)(2,1)S(1)}, /*index=5*/s32[]{:T(128)}) while((s32[]{:T(128)}, bf16[5,192,128]{2,1,0:T(8,128)(2,1)S(1)}, bf16[5,192,128]{2,1,0:T(8,128)(2,1)}, ...), condition=%wide.region_11.12_spmd, body=%wide.region_8.11_spmd.sunk | while | flops 57421440 | bytes 1775941 | solution.py:38
  626.5 1.1 fusion.47
  628.3 1.1 fusion.47
  630.0 1.1 fusion.47
  631.7 1.1 fusion.47
  633.4 1.1 fusion.47
  638.0 8.6 %while.21 = (s32[]{:T(128)}, bf16[5,192,128]{2,1,0:T(8,128)(2,1)S(1)}, bf16[5,192,128]{2,1,0:T(8,128)(2,1)}, bf16[5,576,128]{2,1,0:T(8,128)(2,1)S(1)}, bf16[5,576,128]{2,1,0:T(8,128)(2,1)S(1)}, /*index=5*/s32[]{:T(128)}) while((s32[]{:T(128)}, bf16[5,192,128]{2,1,0:T(8,128)(2,1)S(1)}, bf16[5,192,128]{2,1,0:T(8,128)(2,1)}, ...), condition=%wide.region_21.22_spmd, body=%wide.region_18.21_spmd.sunk | while | flops 57421440 | bytes 1775941 | solution.py:38
  638.0 1.1 fusion.51
  639.8 1.1 fusion.51
  641.5 1.1 fusion.51
  643.2 1.1 fusion.51
  644.9 1.1 fusion.51
  648.3 9.8 %all_to_all.64 = bf16[8,24,640]{2,1,0:T(8,128)(2,1)S(1)} all-to-all(bf16[8,24,640]{2,1,0:T(8,128)(2,1)S(1)} %add_convert_fusion), channel_id=1, replica_groups=mesh['frame'=64,'head'=8] {'head'}, dimensions={0} | all-to-all | bytes 491520 | tf_op jit(solution)/shard_map/all_to_all | solution.py:108
  (103 shorter events, 25.1 us)
Async XLA Ops:
  6.5 8.9 %copy-start.2 = (bf16[192,640]{1,0:T(8,128)(2,1)S(1)}, bf16[192,640]{1,0:T(8,128)(2,1)}, u32[]{:S(2)}) copy-start(bf16[192,640]{1,0:T(8,128)(2,1)} %param.17) | copy-start | bytes 737284
  6.5 9.1 %copy-start.1 = (bf16[192,640]{1,0:T(8,128)(2,1)S(1)}, bf16[192,640]{1,0:T(8,128)(2,1)}, u32[]{:S(2)}) copy-start(bf16[192,640]{1,0:T(8,128)(2,1)} %param.18) | copy-start | bytes 737284
  6.5 26.0 %copy-start.14 = (s32[2]{0:T(128)S(1)}, s32[2]{0:T(128)}, u32[]{:S(2)}) copy-start(s32[2]{0:T(128)} %param.27) | copy-start | bytes 28
  6.5 27.8 %copy-start.8 = (bf16[24,5120]{1,0:T(8,128)(2,1)S(1)}, bf16[24,5120]{1,0:T(8,128)(2,1)}, u32[]{:S(2)}) copy-start(bf16[24,5120]{1,0:T(8,128)(2,1)} %param.24) | copy-start | bytes 737284
  7.7 27.3 %copy-start = (bf16[24,5120]{1,0:T(8,128)(2,1)S(1)}, bf16[24,5120]{1,0:T(8,128)(2,1)}, u32[]{:S(2)}) copy-start(bf16[24,5120]{1,0:T(8,128)(2,1)} %param.22) | copy-start | bytes 737284
  8.9 26.4 %copy-start.3 = (bf16[192,640]{1,0:T(8,128)(2,1)S(1)}, bf16[192,640]{1,0:T(8,128)(2,1)}, u32[]{:S(2)}) copy-start(bf16[192,640]{1,0:T(8,128)(2,1)} %param.19) | copy-start | bytes 737284
  8.9 26.4 %copy-start.12 = (f32[640]{0:T(1024)S(1)}, f32[640]{0:T(1024)}, u32[]{:S(2)}) copy-start(f32[640]{0:T(1024)} %param.21) | copy-start | bytes 7684
  9.6 26.8 %all-to-all-start.1 = ((bf16[24,8,640]{2,0,1:T(8,128)(2,1)}), bf16[24,8,640]{2,0,1:T(8,128)(2,1)S(1)}, u32[]{:S(2)}, u32[]{:S(2)}) async-start(bf16[24,8,640]{2,0,1:T(8,128)(2,1)} %bitcast.76), calls=%async_computation.1 | async-start | bytes 491520 | tf_op jit(solution)/shard_map/all_to_all | solution.py:76
  36.4 9.4 %all-to-all-start.2 = ((bf16[24,8,640]{2,0,1:T(8,128)(2,1)}), bf16[24,8,640]{2,0,1:T(8,128)(2,1)S(1)}, u32[]{:S(2)}, u32[]{:S(2)}) async-start(bf16[24,8,640]{2,0,1:T(8,128)(2,1)} %bitcast.75), calls=%async_computation.2 | async-start | bytes 491520 | tf_op jit(solution)/shard_map/all_to_all | solution.py:77
  39.8 583.3 %all-reduce.4.cloned.1.call-start = ((), (), s32[]{:S(2)}) async-start(), calls=%async_computation.4 | async-start | bytes 5111808 | tf_op jit(solution)/shard_map/psum | solution.py:16
  50.0 0.7 copy-start.11
  50.8 4.3 copy-start.13
  50.8 4.4 copy-start.15
  51.6 9.4 %all-to-all-start = ((bf16[24,8,640]{2,0,1:T(8,128)(2,1)}), bf16[24,8,640]{2,0,1:T(8,128)(2,1)S(1)}, u32[]{:S(2)}, u32[]{:S(2)}) async-start(bf16[24,8,640]{2,0,1:T(8,128)(2,1)} %bitcast.77), calls=%async_computation | async-start | bytes 491520 | tf_op jit(solution)/shard_map/all_to_all | solution.py:75
  624.6 0.9 copy-start.9
  624.6 1.1 copy-start.10
  635.1 1.0 copy-start.6
  635.1 1.1 copy-start.7
  636.5 1.0 copy-start.4
  636.5 1.1 copy-start.5
Sparse Core Ops, SparseCore 0:
  50.2 572.8 all-reduce.3
where the time goes:
time: 669 us; the launch traced here: 666 us
  waiting for transfers between devices  570 us (85%)
  blocking collectives  26.6 us (4%)
  local copies, waits for them, and re-layouts  17.1 us (3%)
  between operations  15.6 us (2%)
  matrix products  14.6 us (2%)
  starting transfers between devices  12.7 us (2%)
  other arithmetic  9.14 us (1%)
    psum x1, waiting for transfers between devices, spread(): return lax.psum(block, axis)  561 us
    psum x1, blocking collectives, body(): sum_q, sum_k = lax.psum((squares(q_high), squares(k_high)), 'head')  16.8 us
  transfers between devices with their start and end apart: 4, of which 3 were waited for; matrix products, arithmetic and copies ran while one was open for 1% of the time, Pallas kernels for 0%

commit v1 on v0

v1 whole, which is shorter than its diff:
```python
import functools
import math

import jax
import jax.numpy as jnp
from jax import lax
from jax.experimental import pallas as pl
from jax.experimental.pallas import tpu as pltpu
from jax.sharding import PartitionSpec as P

HEADS = 40
HD = 128
STEPS = 40
EPS = 1e-06
TOK = 192
W = 640
WIDTH = HEADS * HD
LOCAL = 24
BF = jnp.bfloat16
F32 = jnp.float32
MESH = pl.DeviceIdType.MESH
QSCALE = HD ** (-0.5) * math.log2(math.e)


def kernel(
    kf,
    step_ref,
    q_high,
    k_high,
    v_high,
    gain_qh,
    gain_kh,
    q_low,
    k_low,
    v_low,
    gain_ql,
    gain_kl,
    perm,
    out,
    KV,
    Q,
    OH,
    CH,
    H1R,
    RZ,
    ZC,
    RY,
    SKV,
    RKV,
    SQ,
    RQ,
    SS,
    RS,
    MB,
    RB,
    send_sems,
    sum_sems,
    akv_sems,
    aq_sems,
    back_sems,
    h1_sems,
    rz_sems,
    ry_sems,
    yg_sems,
    ag_sems,
    sb_sems,
):
    f = lax.axis_index("frame")
    h = lax.axis_index("head")
    z = f // 8
    y = (f // 2) % 4
    c = f % 2
    sgn = (1 - 2 * c, 2 * c - 1)

    def at(zz, yy, cc, hh):
        return {"frame": (zz * 4 + yy) * 2 + cc, "head": hh}

    sibling = at(z, y, 1 - c, h)
    zdev = [at((z + s + 8) % 8, y, c, h) for s in sgn]
    ydev = [at(z, (y + j) % 4, c, h) for j in range(4)]
    hidx = [(h + j) % 8 for j in range(8)]
    hdev = [at(z, y, c, hidx[j]) for j in range(8)]

    barrier = pltpu.get_barrier_semaphore()
    partners = [sibling] + zdev + ydev[1:] + hdev[1:]
    for dev in partners:
        pl.semaphore_signal(barrier, inc=1, device_id=dev, device_id_type=MESH)

    count = [0]
    ends = []

    def rcopy(src, dst, rsem, dev, cond=None):
        index = count[0]
        count[0] += 1
        copy = pltpu.make_async_remote_copy(
            src_ref=src,
            dst_ref=dst,
            send_sem=send_sems.at[index],
            recv_sem=rsem,
            device_id=dev,
            device_id_type=MESH,
        )
        if cond is None:
            copy.start()
        else:
            pl.when(cond)(copy.start)
        ends.append((copy, cond))

    def arrived(dst, rsem):
        pltpu.make_async_remote_copy(
            src_ref=dst,
            dst_ref=dst,
            send_sem=send_sems.at[0],
            recv_sem=rsem,
            device_id=sibling,
            device_id_type=MESH,
        ).wait_recv()

    def rows_sum(ref):
        x = ref[...].astype(F32)
        x = x * x
        hi = x.astype(BF)
        lo = (x - hi.astype(F32)).astype(BF)
        ones = jnp.ones((8, W), BF)
        dims = (((1,), (1,)), ((), ()))
        return lax.dot_general(ones, hi, dims, preferred_element_type=F32) + lax.dot_general(
            ones, lo, dims, preferred_element_type=F32
        )

    eight = lax.broadcasted_iota(jnp.int32, (8, TOK), 0)
    SS[...] = jnp.where(eight < 4, rows_sum(q_high), rows_sum(k_high))
    RS[h] = SS[...]
    KV[0, 1, 0:TOK] = v_high[...]

    pl.semaphore_wait(barrier, len(partners))

    for j in range(1, 8):
        rcopy(SS, RS.at[h], sum_sems.at[h], hdev[j])

    def h1_rows(rh, core):
        return pl.ds(pl.multiple_of(96 * rh + 48 * core, 16), 48)

    def h1_send(e, kv):
        for rh in range(2):
            rcopy(
                KV.at[e, kv, h1_rows(rh, 1 - c)],
                H1R.at[e, kv, rh],
                h1_sems.at[e, kv, rh],
                sibling,
            )

    h1_send(0, 1)

    def factor(ref):
        x = ref[...].astype(F32)
        return lax.rsqrt(jnp.sum(x * x, axis=1, keepdims=True) / WIDTH + EPS)

    fk = factor(k_low)
    for p in range(8):
        cols = slice(W * p, W * p + W)
        kn = k_low[:, cols].astype(F32) * fk * gain_kl[:, cols]
        SKV[p] = jnp.concatenate([kn, v_low[:, cols].astype(F32)], axis=0).astype(BF)
    RKV[h] = SKV[h]
    for j in range(1, 8):
        rcopy(SKV.at[hidx[j]], RKV.at[h], akv_sems.at[h], hdev[j])
    fq = factor(q_low)
    for p in range(8):
        cols = slice(W * p, W * p + W)
        qn = q_low[:, cols].astype(F32) * (fq * QSCALE) * gain_ql[:, cols]
        SQ[p] = jnp.concatenate([qn, jnp.zeros((8, W), F32)], axis=0).astype(BF)
    RQ[h] = SQ[h]
    for j in range(1, 8):
        rcopy(SQ.at[hidx[j]], RQ.at[h], aq_sems.at[h], hdev[j])

    for j in range(1, 8):
        arrived(RS.at[hidx[j]], sum_sems.at[hidx[j]])
    total = RS[0]
    for p in range(1, 8):
        total = total + RS[p]
    total = lax.rsqrt(total / WIDTH + EPS)

    def spread_rows(row):
        pick = jnp.where(lax.broadcasted_iota(jnp.int32, (8, HD), 0) == row, 1.0, 0.0)
        return lax.dot_general(
            total,
            pick,
            (((0,), (0,)), ((), ())),
            precision=lax.Precision.HIGHEST,
            preferred_element_type=F32,
        )

    kfac = spread_rows(4)
    for g in range(5):
        cols = slice(HD * g, HD * g + HD)
        KV[0, 0, 0:TOK, cols] = (k_high[:, cols].astype(F32) * kfac * gain_kh[:, cols]).astype(BF)
    h1_send(0, 0)
    qfac = spread_rows(0) * QSCALE
    hot = jnp.where(lax.broadcasted_iota(jnp.int32, (TOK, TOK), 0) == perm[...], 1.0, 0.0).astype(BF)
    for g in range(5):
        cols = slice(HD * g, HD * g + HD)
        qn = (q_high[:, cols].astype(F32) * qfac * gain_qh[:, cols]).astype(BF)
        Q[0, :, cols] = lax.dot_general(
            hot, qn, (((0,), (0,)), ((), ())), preferred_element_type=F32
        ).astype(BF)

    def place(e, o, k, n=1):
        row = TOK + TOK * (o // 4) + 96 * (o % 2) + 48 * c + 16 * k
        return KV.at[e, (o // 2) % 2, pl.ds(pl.multiple_of(row, 16), 16 * n)]

    def chunk(k):
        return pl.ds(16 * k, 16)

    far = ((0, 2), (1,))

    def gather_pair(e):
        for kv in range(2):
            for rh in range(2):
                arrived(H1R.at[e, kv, rh], h1_sems.at[e, kv, rh])
                mine = KV[e, kv, h1_rows(rh, c)]
                other = H1R[e, kv, rh]
                for s in range(2):
                    CH[e, s * 4 + kv * 2 + rh] = jnp.where(kf[s] % 2 == c, mine, other)

    def slot_of(o):
        return jnp.where(o // 4 == 0, kf[0], kf[1])

    def rs_send(e, t):
        for k in (0, 2, 1):
            for d in range(2):
                o = (z + sgn[d] * (5 - t) + 8) % 8
                if t == 1 and k not in far[d]:
                    continue
                if t == 1 or (t == 2 and k not in far[d]):
                    src = CH.at[e, o, chunk(k)]
                else:
                    got = RZ.at[e, d, t - 2, chunk(k)]
                    arrived(got, rz_sems.at[e, d, t - 2, k])
                    got[...] = jnp.where(slot_of(o) // 8 == z, CH[e, o, chunk(k)], got[...])
                    src = got
                rcopy(src, RZ.at[e, d, t - 1, chunk(k)], rz_sems.at[e, d, t - 1, k], zdev[d])

    def yowner(k):
        return (k + z + 2 * c) % 4

    def y_send(e):
        root = slot_of(z) // 8
        away = ((z - root) * sgn[0] + 8) % 8
        for k in range(3):
            for d in range(2):
                arrived(RZ.at[e, d, 3, chunk(k)], rz_sems.at[e, d, 3, k])
            limit = 5 if k in far[0] else 4
            mixed = jnp.where(away < limit, RZ[e, 0, 3, chunk(k)], RZ[e, 1, 3, chunk(k)])
            ZC[e, k] = jnp.where(away == 0, CH[e, z, chunk(k)], mixed)
            yo = yowner(k)
            rcopy(
                ZC.at[e, k], RY.at[e, y], ry_sems.at[e, y], at(z, yo, c, h), cond=yo != y
            )

    def y_own(e):
        kme = (y - z - 2 * c + 12) % 4
        own = kme < 3
        kme = jnp.minimum(kme, 2)

        @pl.when(own)
        def _():
            for j in range(1, 4):
                yy = (y + j) % 4
                arrived(RY.at[e, yy], ry_sems.at[e, yy])
            RY[e, y] = ZC[e, kme]
            root = (slot_of(z) // 2) % 4
            value = RY[e, 0]
            for yy in range(1, 4):
                value = jnp.where(root == yy, RY[e, yy], value)
            place(e, z, kme)[...] = value

        for j in range(1, 4):
            rcopy(place(e, z, kme), place(e, z, kme), yg_sems.at[e, kme], ydev[j], cond=own)

    def ag_send(e, j):
        for k in (0, 2, 1):
            if j == 1:

                @pl.when(yowner(k) != y)
                def _():
                    arrived(place(e, z, k), yg_sems.at[e, k])

            for d in range(2):
                o = (z - sgn[d] * (j - 1) + 8) % 8
                if j > 1:
                    arrived(place(e, o, k), ag_sems.at[e, d, j - 2, k])
                if j == 4 and k not in far[d]:
                    continue
                rcopy(place(e, o, k), place(e, o, k), ag_sems.at[e, d, j - 1, k], zdev[d])
        for d in range(2 if j > 1 else 1):
            o = (z - sgn[d] * (j - 1) + 8) % 8
            i = 2 * (j - 1) + d - (1 if j > 1 else 0)
            rcopy(place(e, o, 0, 3), place(e, o, 0, 3), sb_sems.at[e, i], sibling)

    def ag_last(e):
        o = (z + 4) % 8
        for d in range(2):
            for k in far[d]:
                arrived(place(e, o, k), ag_sems.at[e, d, 3, k])
                rcopy(place(e, o, k), place(e, o, k), sb_sems.at[e, 7 + k], sibling)

    def sib_place(e, o, k, n=1):
        row = TOK + TOK * (o // 4) + 96 * (o % 2) + 48 * (1 - c) + 16 * k
        return KV.at[e, (o // 2) % 2, pl.ds(pl.multiple_of(row, 16), 16 * n)]

    def sib_wait(e):
        sib_sgn = (sgn[1], sgn[0])
        for j in range(1, 5):
            for d in range(2 if j > 1 else 1):
                o = (z - sib_sgn[d] * (j - 1) + 8) % 8
                i = 2 * (j - 1) + d - (1 if j > 1 else 0)
                arrived(sib_place(e, o, 0, 3), sb_sems.at[e, i])
        o = (z + 4) % 8
        for k in range(3):
            arrived(sib_place(e, o, k), sb_sems.at[e, 7 + k])

    lam = step_ref[0].astype(F32) / STEPS

    def heads(e):
        def one(g, carry):
            cols = pl.ds(pl.multiple_of(g * HD, HD), HD)
            q = Q[e, :, cols]
            keys = KV[e, 0, :, cols]
            vals = KV[e, 1, :, cols]
            s = lax.dot_general(q, keys, (((1,), (1,)), ((), ())), preferred_element_type=F32)
            p = jnp.exp2(s - jnp.max(s, axis=1, keepdims=True)).astype(BF)
            both = jnp.concatenate([vals, jnp.ones((3 * TOK, HD), BF)], axis=1)
            o = lax.dot_general(p, both, (((1,), (0,)), ((), ())), preferred_element_type=F32)
            o = (o[:, :HD] / o[:, HD:]).astype(BF)
            if e == 0:
                OH[:, cols] = o
            else:
                mixed = (1.0 - lam) * OH[:, cols].astype(F32) + lam * o.astype(F32)
                pad = jnp.zeros((8, HD), F32)
                for p8 in range(8):
                    rows = mixed[LOCAL * p8 : LOCAL * p8 + LOCAL]
                    MB[p8, :, cols] = jnp.concatenate([rows, pad], axis=0).astype(BF)
            return carry

        lax.fori_loop(0, 5, one, 0)

    def low_keys():
        for j in range(1, 8):
            arrived(RKV.at[hidx[j]], akv_sems.at[hidx[j]])
        for p in range(4):
            a = RKV[2 * p].astype(F32)
            b = RKV[2 * p + 1].astype(F32)
            rows = slice(48 * p, 48 * p + 48)
            KV[1, 0, rows] = jnp.concatenate([a[:LOCAL], b[:LOCAL]], axis=0).astype(BF)
            KV[1, 1, rows] = jnp.concatenate([a[LOCAL:], b[LOCAL:]], axis=0).astype(BF)

    def low_queries():
        for j in range(1, 8):
            arrived(RQ.at[hidx[j]], aq_sems.at[hidx[j]])
        for p in range(4):
            a = RQ[2 * p].astype(F32)
            b = RQ[2 * p + 1].astype(F32)
            Q[1, 48 * p : 48 * p + 48] = jnp.concatenate([a[:LOCAL], b[:LOCAL]], axis=0).astype(BF)

    gather_pair(0)
    rs_send(0, 1)
    rs_send(0, 2)
    rs_send(0, 3)
    low_keys()
    h1_send(1, 0)
    h1_send(1, 1)
    rs_send(0, 4)
    gather_pair(1)
    rs_send(1, 1)
    y_send(0)
    rs_send(1, 2)
    y_own(0)
    rs_send(1, 3)
    ag_send(0, 1)
    rs_send(1, 4)
    ag_send(0, 2)
    y_send(1)
    ag_send(0, 3)
    y_own(1)
    ag_send(0, 4)
    ag_send(1, 1)
    ag_last(0)
    low_queries()
    ag_send(1, 2)
    sib_wait(0)
    ag_send(1, 3)
    ag_send(1, 4)
    heads(0)
    ag_last(1)
    sib_wait(1)
    heads(1)

    RB[h] = MB[h]
    for j in range(1, 8):
        rcopy(MB.at[hidx[j]], RB.at[h], back_sems.at[h], hdev[j])
    for j in range(1, 8):
        arrived(RB.at[hidx[j]], back_sems.at[hidx[j]])
    for p in range(8):
        out[:, W * p : W * p + W] = RB[p, 0:LOCAL]

    for copy, cond in ends:
        if cond is None:
            copy.wait_send()
        else:
            pl.when(cond)(copy.wait_send)


def body(
    q_high,
    k_high,
    v_high,
    gain_qh,
    gain_kh,
    q_low,
    k_low,
    v_low,
    gain_ql,
    gain_kl,
    keyframes,
    switch_step,
    permutation,
):
    smem = pl.BlockSpec(memory_space=pltpu.SMEM)
    vmem = pl.BlockSpec(memory_space=pltpu.VMEM)
    dma = pltpu.SemaphoreType.DMA
    return pl.pallas_call(
        kernel,
        out_shape=jax.ShapeDtypeStruct((LOCAL, WIDTH), BF),
        in_specs=[smem, smem] + [vmem] * 11,
        out_specs=vmem,
        scratch_shapes=[
            pltpu.VMEM((2, 2, 3 * TOK, W), BF),
            pltpu.VMEM((2, TOK, W), BF),
            pltpu.VMEM((TOK, W), BF),
            pltpu.VMEM((2, 8, 48, W), BF),
            pltpu.VMEM((2, 2, 2, 48, W), BF),
            pltpu.VMEM((2, 2, 4, 48, W), BF),
            pltpu.VMEM((2, 3, 16, W), BF),
            pltpu.VMEM((2, 4, 16, W), BF),
            pltpu.VMEM((8, 48, W), BF),
            pltpu.VMEM((8, 48, W), BF),
            pltpu.VMEM((8, 32, W), BF),
            pltpu.VMEM((8, 32, W), BF),
            pltpu.VMEM((8, TOK), F32),
            pltpu.VMEM((8, 8, TOK), F32),
            pltpu.VMEM((8, 32, W), BF),
            pltpu.VMEM((8, 32, W), BF),
            dma((200,)),
            dma((8,)),
            dma((8,)),
            dma((8,)),
            dma((8,)),
            dma((2, 2, 2)),
            dma((2, 2, 4, 3)),
            dma((2, 4)),
            dma((2, 4)),
            dma((2, 2, 4, 3)),
            dma((2, 10)),
        ],
        compiler_params=pltpu.CompilerParams(
            collective_id=0, has_side_effects=True, vmem_limit_bytes=40 * 1024 * 1024
        ),
    )(
        keyframes,
        switch_step,
        q_high,
        k_high,
        v_high,
        gain_qh.reshape(1, W),
        gain_kh.reshape(1, W),
        q_low,
        k_low,
        v_low,
        gain_ql.reshape(1, WIDTH),
        gain_kl.reshape(1, WIDTH),
        permutation.reshape(1, TOK),
    )


def solution(mesh):
    return jax.shard_map(
        body,
        mesh=mesh,
        in_specs=(
            P("frame", "head"),
            P("frame", "head"),
            P("frame", "head"),
            P("head"),
            P("head"),
            P(("frame", "head"), None),
            P(("frame", "head"), None),
            P(("frame", "head"), None),
            P(),
            P(),
            P(),
            P(),
            P(),
        ),
        out_specs=P(("frame", "head"), None),
        check_vma=False,
    )
```

time: 669 us -> 95.1 us (0.14)
  waiting for transfers between devices: 570 us -> 0 us
  Pallas kernels: 0 us -> 84.8 us
  blocking collectives: 26.6 us -> 0 us
  between operations: 15.6 us -> 0.68 us
  matrix products: 14.6 us -> 0 us
  starting transfers between devices: 12.7 us -> 0 us
  other arithmetic: 9.14 us -> 0 us
  local copies, waits for them, and re-layouts: 17.1 us -> 9.16 us
    psum x1 -> x0, waiting for transfers between devices: 561 us -> none  [spread(): return lax.psum(block, axis)]
    pallas_call x0 -> x1, Pallas kernels: none -> 84.8 us  [body(): pl.pallas_call(kernel, out_shape=jax.ShapeDtypeStruct((LOCAL, WIDTH), BF)...]
    psum x1 -> x0, blocking collectives: 16.8 us -> none  [body(): sum_q, sum_k = lax.psum((squares(q_high), squares(k_high)), 'head')]
    dot_general x20 -> x0, matrix products: 14.6 us -> none  [the longest x10 11.3 us: one_head(): jnp.einsum('qd,kd->qk', qpart, kpart, preferred_element_type=jnp.float32)]
    all_to_all x3 -> x0, starting transfers between devices: 12.7 us -> none  [the longest x1 5.86 us: body(): lax.all_to_all(kn_low, 'head', split_axis=1, concat_axis=0, tiled=True)]
    all_to_all x1 -> x0, blocking collectives: 9.77 us -> none  [body(): lax.all_to_all(mixed, 'head', split_axis=0, concat_axis=1, tiled=True)]
    all_to_all x3 -> x0, waiting for transfers between devices: 8.62 us -> none  [the longest x1 5.21 us: body(): lax.all_to_all(v_low, 'head', split_axis=1, concat_axis=0, tiled=True)]
  transfers between devices with their start and end apart: 4 -> 0, of which waited for: 3 -> 0; matrix products, arithmetic and copies ran while one was open for 1% -> 0% of each run, Pallas kernels for 0% -> 0%
where the time goes in v1:
time: 95.1 us; the launch traced here: 94.6 us
  Pallas kernels  84.8 us (89%)
  local copies, waits for them, and re-layouts  9.16 us (10%)
    pallas_call x1, Pallas kernels, body(): pl.pallas_call(kernel, out_shape=jax.ShapeDtypeStruct((LOCAL, WIDTH), BF)...  84.8 us
    unnamed x21, local copies, waits for them, and re-layouts  7.77 us

profile of v1, /device:TPU:1, one launch (start us, length us, event | category | flops | bytes accessed | tf_op | source)
XLA Modules:
  0.0 94.6 jit_solution(3994635107318727772)
XLA Ops:
  0.0 0.0 copy-start.6
  0.7 0.7 reshape.15.gain_qh
  1.4 0.0 copy-start.9
  1.4 0.7 reshape.16.gain_kh
  2.1 0.0 copy-done.6
  2.1 0.0 copy-done.9
  2.1 0.0 copy-start
  2.1 0.9 copy-done
  3.0 0.0 copy-start.1
  3.0 0.9 copy-done.1
  4.0 0.0 copy-start.2
  4.0 0.9 copy-done.2
  4.9 0.0 copy-start.3
  4.9 0.9 copy-done.3
  5.8 0.0 copy-start.4
  5.8 0.9 copy-done.4
  6.8 0.0 copy-start.5
  6.8 0.9 copy-done.5
  7.7 0.0 copy-start.7
  7.7 0.7 copy-done.7
  8.5 0.0 copy-start.8
  8.5 0.7 copy-done.8
  9.1 84.8 %shard_map.127 = bf16[24,5120]{1,0:T(8,128)(2,1)S(1)} custom-call(s32[2]{0:T(128)S(1)} %copy-done.9, s32[1]{0:T(128)S(6)} %copy.15.step_ref, bf16[192,640]{1,0:T(8,128)(2,1)S(1)} %copy-done, bf16[192,640]{1,0:T(8,128)(2,1)S(1)} %copy-done.1, bf16[192,640]{1,0:T(8,128)(2,1)S(1)} %copy-done.2, f32[1,640]{1,0:T(1,128)S(1)} %reshape.15.gain_qh, ...), custom_call_target="tpu_custom_call" | custom-call | tf_op jit(solution)/shard_map/pallas_call | solution.py:430
  94.0 0.7 copy.16
Async XLA Ops:
  0.0 2.1 %copy-start.6 = (f32[5120]{0:T(1024)S(1)}, f32[5120]{0:T(1024)}, u32[]{:S(2)}) copy-start(f32[5120]{0:T(1024)} %param.21) | copy-start | bytes 61444
  1.4 0.7 copy-start.9
  2.1 0.9 copy-start
  3.0 0.9 copy-start.1
  4.0 0.9 copy-start.2
  4.9 0.9 copy-start.3
  5.8 0.9 copy-start.4
  6.8 0.9 copy-start.5
  7.7 0.7 copy-start.7
  8.5 0.7 copy-start.8

commit v2 on v1

--- a/solution.py
+++ b/solution.py
@@ -25,18 +25,28 @@
 def kernel(
     kf,
     step_ref,
+    q_high_hbm,
+    k_high_hbm,
+    v_high_hbm,
+    gain_qh_hbm,
+    gain_kh_hbm,
+    q_low_hbm,
+    k_low_hbm,
+    v_low_hbm,
+    gain_ql_hbm,
+    gain_kl_hbm,
+    perm_hbm,
+    out,
     q_high,
     k_high,
-    v_high,
-    gain_qh,
-    gain_kh,
     q_low,
     k_low,
     v_low,
+    gain_qh,
+    gain_kh,
     gain_ql,
     gain_kl,
     perm,
-    out,
     KV,
     Q,
     OH,
@@ -53,6 +63,7 @@
     RS,
     MB,
     RB,
+    load_sems,
     send_sems,
     sum_sems,
     akv_sems,
@@ -77,12 +88,30 @@
 
     sibling = at(z, y, 1 - c, h)
     zdev = [at((z + s + 8) % 8, y, c, h) for s in sgn]
+    zdev2 = [at((z + 2 * s + 8) % 8, y, c, h) for s in sgn]
     ydev = [at(z, (y + j) % 4, c, h) for j in range(4)]
     hidx = [(h + j) % 8 for j in range(8)]
     hdev = [at(z, y, c, hidx[j]) for j in range(8)]
 
+    loads = []
+    for src, dst in (
+        (k_high_hbm, k_high),
+        (q_high_hbm, q_high),
+        (v_high_hbm, KV.at[0, 1, pl.ds(0, TOK)]),
+        (k_low_hbm, k_low),
+        (v_low_hbm, v_low),
+        (gain_kl_hbm, gain_kl),
+        (q_low_hbm, q_low),
+        (gain_ql_hbm, gain_ql),
+        (gain_kh_hbm, gain_kh),
+        (gain_qh_hbm, gain_qh),
+        (perm_hbm, perm),
+    ):
+        loads.append(pltpu.make_async_copy(src, dst, load_sems.at[len(loads)]))
+        loads[-1].start()
+
     barrier = pltpu.get_barrier_semaphore()
-    partners = [sibling] + zdev + ydev[1:] + hdev[1:]
+    partners = [sibling] + zdev + zdev2 + ydev[1:] + hdev[1:]
     for dev in partners:
         pl.semaphore_signal(barrier, inc=1, device_id=dev, device_id_type=MESH)
 
@@ -127,10 +156,12 @@
             ones, lo, dims, preferred_element_type=F32
         )
 
+    loads[0].wait()
+    loads[1].wait()
     eight = lax.broadcasted_iota(jnp.int32, (8, TOK), 0)
     SS[...] = jnp.where(eight < 4, rows_sum(q_high), rows_sum(k_high))
     RS[h] = SS[...]
-    KV[0, 1, 0:TOK] = v_high[...]
+    loads[2].wait()
 
     pl.semaphore_wait(barrier, len(partners))
 
@@ -155,18 +186,22 @@
         x = ref[...].astype(F32)
         return lax.rsqrt(jnp.sum(x * x, axis=1, keepdims=True) / WIDTH + EPS)
 
+    for i in (3, 4, 5):
+        loads[i].wait()
     fk = factor(k_low)
     for p in range(8):
         cols = slice(W * p, W * p + W)
-        kn = k_low[:, cols].astype(F32) * fk * gain_kl[:, cols]
+        kn = k_low[:, cols].astype(F32) * fk * gain_kl[cols].reshape(1, W)
         SKV[p] = jnp.concatenate([kn, v_low[:, cols].astype(F32)], axis=0).astype(BF)
     RKV[h] = SKV[h]
     for j in range(1, 8):
         rcopy(SKV.at[hidx[j]], RKV.at[h], akv_sems.at[h], hdev[j])
+    loads[6].wait()
+    loads[7].wait()
     fq = factor(q_low)
     for p in range(8):
         cols = slice(W * p, W * p + W)
-        qn = q_low[:, cols].astype(F32) * (fq * QSCALE) * gain_ql[:, cols]
+        qn = q_low[:, cols].astype(F32) * (fq * QSCALE) * gain_ql[cols].reshape(1, W)
         SQ[p] = jnp.concatenate([qn, jnp.zeros((8, W), F32)], axis=0).astype(BF)
     RQ[h] = SQ[h]
     for j in range(1, 8):
@@ -189,16 +224,18 @@
             preferred_element_type=F32,
         )
 
+    for i in (8, 9, 10):
+        loads[i].wait()
     kfac = spread_rows(4)
     for g in range(5):
         cols = slice(HD * g, HD * g + HD)
-        KV[0, 0, 0:TOK, cols] = (k_high[:, cols].astype(F32) * kfac * gain_kh[:, cols]).astype(BF)
+        KV[0, 0, 0:TOK, cols] = (k_high[:, cols].astype(F32) * kfac * gain_kh[cols].reshape(1, HD)).astype(BF)
     h1_send(0, 0)
     qfac = spread_rows(0) * QSCALE
-    hot = jnp.where(lax.broadcasted_iota(jnp.int32, (TOK, TOK), 0) == perm[...], 1.0, 0.0).astype(BF)
+    hot = jnp.where(lax.broadcasted_iota(jnp.int32, (TOK, TOK), 0) == perm[...].reshape(1, TOK), 1.0, 0.0).astype(BF)
     for g in range(5):
         cols = slice(HD * g, HD * g + HD)
-        qn = (q_high[:, cols].astype(F32) * qfac * gain_qh[:, cols]).astype(BF)
+        qn = (q_high[:, cols].astype(F32) * qfac * gain_qh[cols].reshape(1, HD)).astype(BF)
         Q[0, :, cols] = lax.dot_general(
             hot, qn, (((0,), (0,)), ((), ())), preferred_element_type=F32
         ).astype(BF)
@@ -207,10 +244,10 @@
         row = TOK + TOK * (o // 4) + 96 * (o % 2) + 48 * c + 16 * k
         return KV.at[e, (o // 2) % 2, pl.ds(pl.multiple_of(row, 16), 16 * n)]
 
-    def chunk(k):
-        return pl.ds(16 * k, 16)
-
-    far = ((0, 2), (1,))
+    def chunk(k, n=1):
+        return pl.ds(16 * k, 16 * n)
+
+    far = ((0, 2), (2, 1))
 
     def gather_pair(e):
         for kv in range(2):
@@ -224,40 +261,52 @@
     def slot_of(o):
         return jnp.where(o // 4 == 0, kf[0], kf[1])
 
-    def rs_send(e, t):
-        for k in (0, 2, 1):
-            for d in range(2):
-                o = (z + sgn[d] * (5 - t) + 8) % 8
-                if t == 1 and k not in far[d]:
-                    continue
-                if t == 1 or (t == 2 and k not in far[d]):
-                    src = CH.at[e, o, chunk(k)]
-                else:
-                    got = RZ.at[e, d, t - 2, chunk(k)]
-                    arrived(got, rz_sems.at[e, d, t - 2, k])
-                    got[...] = jnp.where(slot_of(o) // 8 == z, CH[e, o, chunk(k)], got[...])
-                    src = got
-                rcopy(src, RZ.at[e, d, t - 1, chunk(k)], rz_sems.at[e, d, t - 1, k], zdev[d])
+    def rs_first(e):
+        for d in range(2):
+            k, n = far[d]
+            o3, o4, o1 = ((z + i * sgn[d] + 8) % 8 for i in (3, 4, 1))
+            rcopy(CH.at[e, o3], RZ.at[e, d, 0], rz_sems.at[e, d, 0], zdev[d])
+            rcopy(CH.at[e, o4, chunk(k, n)], RZ.at[e, d, 1, chunk(k, n)], rz_sems.at[e, d, 1], zdev2[d])
+        for d in range(2):
+            o1 = (z + sgn[d] + 8) % 8
+            rcopy(CH.at[e, o1], RZ.at[e, d, 2], rz_sems.at[e, d, 2], zdev[d])
+
+    def rs_second(e):
+        for d in range(2):
+            k, n = far[d]
+            o2 = (z + 2 * sgn[d] + 8) % 8
+            away = ((z - slot_of(o2) // 8) * sgn[d] + 8) % 8
+            arrived(RZ.at[e, d, 0], rz_sems.at[e, d, 0])
+            arrived(RZ.at[e, d, 1, chunk(k, n)], rz_sems.at[e, d, 1])
+            RZ[e, d, 0] = jnp.where(away == 0, CH[e, o2], RZ[e, d, 0])
+            RZ[e, d, 0, chunk(k, n)] = jnp.where(
+                away == 2, RZ[e, d, 1, chunk(k, n)], RZ[e, d, 0, chunk(k, n)]
+            )
+            rcopy(RZ.at[e, d, 0], RZ.at[e, d, 3], rz_sems.at[e, d, 3], zdev2[d])
 
     def yowner(k):
-        return (k + z + 2 * c) % 4
+        return (k + 2 * c) % 4
 
     def y_send(e):
         root = slot_of(z) // 8
         away = ((z - root) * sgn[0] + 8) % 8
+        for d in range(2):
+            arrived(RZ.at[e, d, 2], rz_sems.at[e, d, 2])
+        for d in range(2):
+            arrived(RZ.at[e, d, 3], rz_sems.at[e, d, 3])
         for k in range(3):
-            for d in range(2):
-                arrived(RZ.at[e, d, 3, chunk(k)], rz_sems.at[e, d, 3, k])
-            limit = 5 if k in far[0] else 4
-            mixed = jnp.where(away < limit, RZ[e, 0, 3, chunk(k)], RZ[e, 1, 3, chunk(k)])
-            ZC[e, k] = jnp.where(away == 0, CH[e, z, chunk(k)], mixed)
+            limit = 5 if k < far[0][1] else 4
+            value = jnp.where(away == 1, RZ[e, 0, 2, chunk(k)], RZ[e, 0, 3, chunk(k)])
+            value = jnp.where(away >= limit, RZ[e, 1, 3, chunk(k)], value)
+            value = jnp.where(away == 7, RZ[e, 1, 2, chunk(k)], value)
+            ZC[e, k] = jnp.where(away == 0, CH[e, z, chunk(k)], value)
             yo = yowner(k)
             rcopy(
                 ZC.at[e, k], RY.at[e, y], ry_sems.at[e, y], at(z, yo, c, h), cond=yo != y
             )
 
     def y_own(e):
-        kme = (y - z - 2 * c + 12) % 4
+        kme = (y - 2 * c + 4) % 4
         own = kme < 3
         kme = jnp.minimum(kme, 2)
 
@@ -276,47 +325,60 @@
         for j in range(1, 4):
             rcopy(place(e, z, kme), place(e, z, kme), yg_sems.at[e, kme], ydev[j], cond=own)
 
-    def ag_send(e, j):
-        for k in (0, 2, 1):
-            if j == 1:
-
-                @pl.when(yowner(k) != y)
-                def _():
-                    arrived(place(e, z, k), yg_sems.at[e, k])
-
-            for d in range(2):
-                o = (z - sgn[d] * (j - 1) + 8) % 8
-                if j > 1:
-                    arrived(place(e, o, k), ag_sems.at[e, d, j - 2, k])
-                if j == 4 and k not in far[d]:
-                    continue
-                rcopy(place(e, o, k), place(e, o, k), ag_sems.at[e, d, j - 1, k], zdev[d])
-        for d in range(2 if j > 1 else 1):
-            o = (z - sgn[d] * (j - 1) + 8) % 8
-            i = 2 * (j - 1) + d - (1 if j > 1 else 0)
-            rcopy(place(e, o, 0, 3), place(e, o, 0, 3), sb_sems.at[e, i], sibling)
+    def sib_send(e, o, k, n, i):
+        rcopy(place(e, o, k, n), place(e, o, k, n), sb_sems.at[e, i], sibling)
+
+    def ag_first(e):
+        for k in range(3):
+
+            @pl.when(yowner(k) != y)
+            def _():
+                arrived(place(e, z, k), yg_sems.at[e, k])
+
+        piece = place(e, z, 0, 3)
+        for d in range(2):
+            rcopy(piece, piece, ag_sems.at[e, d, 1], zdev2[d])
+        for d in range(2):
+            rcopy(piece, piece, ag_sems.at[e, d, 0], zdev[d])
+        sib_send(e, z, 0, 3, 0)
+
+    def ag_second(e):
+        for d in range(2):
+            k, n = far[d]
+            o = (z - 2 * sgn[d] + 8) % 8
+            piece = place(e, o, 0, 3)
+            arrived(piece, ag_sems.at[e, d, 1])
+            rcopy(piece, piece, ag_sems.at[e, d, 2], zdev[d])
+            rcopy(place(e, o, k, n), place(e, o, k, n), ag_sems.at[e, d, 3], zdev2[d])
+            sib_send(e, o, 0, 3, 1 + d)
+        for d in range(2):
+            o = (z - sgn[d] + 8) % 8
+            arrived(place(e, o, 0, 3), ag_sems.at[e, d, 0])
+            sib_send(e, o, 0, 3, 3 + d)
 
     def ag_last(e):
+        for d in range(2):
+            o = (z - 3 * sgn[d] + 8) % 8
+            arrived(place(e, o, 0, 3), ag_sems.at[e, d, 2])
+            sib_send(e, o, 0, 3, 5 + d)
         o = (z + 4) % 8
         for d in range(2):
-            for k in far[d]:
-                arrived(place(e, o, k), ag_sems.at[e, d, 3, k])
-                rcopy(place(e, o, k), place(e, o, k), sb_sems.at[e, 7 + k], sibling)
-
-    def sib_place(e, o, k, n=1):
-        row = TOK + TOK * (o // 4) + 96 * (o % 2) + 48 * (1 - c) + 16 * k
-        return KV.at[e, (o // 2) % 2, pl.ds(pl.multiple_of(row, 16), 16 * n)]
+            k, n = far[d]
+            arrived(place(e, o, k, n), ag_sems.at[e, d, 3])
+            sib_send(e, o, k, n, 7 + d)
 
     def sib_wait(e):
-        sib_sgn = (sgn[1], sgn[0])
-        for j in range(1, 5):
-            for d in range(2 if j > 1 else 1):
-                o = (z - sib_sgn[d] * (j - 1) + 8) % 8
-                i = 2 * (j - 1) + d - (1 if j > 1 else 0)
-                arrived(sib_place(e, o, 0, 3), sb_sems.at[e, i])
-        o = (z + 4) % 8
-        for k in range(3):
-            arrived(sib_place(e, o, k), sb_sems.at[e, 7 + k])
+        def place_sib(o, k, n):
+            row = TOK + TOK * (o // 4) + 96 * (o % 2) + 48 * (1 - c) + 16 * k
+            return KV.at[e, (o // 2) % 2, pl.ds(pl.multiple_of(row, 16), 16 * n)]
+
+        arrived(place_sib(z, 0, 3), sb_sems.at[e, 0])
+        for d in range(2):
+            for base, dist in ((1, 2), (3, 1), (5, 3)):
+                o = (z - dist * sgn[1 - d] + 8) % 8
+                arrived(place_sib(o, 0, 3), sb_sems.at[e, base + d])
+            k, n = far[d]
+            arrived(place_sib((z + 4) % 8, k, n), sb_sems.at[e, 7 + d])
 
     lam = step_ref[0].astype(F32) / STEPS
 
@@ -362,33 +424,25 @@
             Q[1, 48 * p : 48 * p + 48] = jnp.concatenate([a[:LOCAL], b[:LOCAL]], axis=0).astype(BF)
 
     gather_pair(0)
-    rs_send(0, 1)
-    rs_send(0, 2)
-    rs_send(0, 3)
+    rs_first(0)
     low_keys()
     h1_send(1, 0)
     h1_send(1, 1)
-    rs_send(0, 4)
+    rs_second(0)
     gather_pair(1)
-    rs_send(1, 1)
+    rs_first(1)
     y_send(0)
-    rs_send(1, 2)
+    rs_second(1)
     y_own(0)
-    rs_send(1, 3)
-    ag_send(0, 1)
-    rs_send(1, 4)
-    ag_send(0, 2)
+    ag_first(0)
+    low_queries()
     y_send(1)
-    ag_send(0, 3)
+    ag_second(0)
     y_own(1)
-    ag_send(0, 4)
-    ag_send(1, 1)
     ag_last(0)
-    low_queries()
-    ag_send(1, 2)
+    ag_first(1)
     sib_wait(0)
-    ag_send(1, 3)
-    ag_send(1, 4)
+    ag_second(1)
     heads(0)
     ag_last(1)
     sib_wait(1)
@@ -426,13 +480,24 @@
 ):
     smem = pl.BlockSpec(memory_space=pltpu.SMEM)
     vmem = pl.BlockSpec(memory_space=pltpu.VMEM)
+    hbm = pl.BlockSpec(memory_space=pl.ANY)
     dma = pltpu.SemaphoreType.DMA
     return pl.pallas_call(
         kernel,
         out_shape=jax.ShapeDtypeStruct((LOCAL, WIDTH), BF),
-        in_specs=[smem, smem] + [vmem] * 11,
+        in_specs=[smem, smem] + [hbm] * 11,
         out_specs=vmem,
         scratch_shapes=[
+            pltpu.VMEM((TOK, W), BF),
+            pltpu.VMEM((TOK, W), BF),
+            pltpu.VMEM((LOCAL, WIDTH), BF),
+            pltpu.VMEM((LOCAL, WIDTH), BF),
+            pltpu.VMEM((LOCAL, WIDTH), BF),
+            pltpu.VMEM((W,), F32),
+            pltpu.VMEM((W,), F32),
+            pltpu.VMEM((WIDTH,), F32),
+            pltpu.VMEM((WIDTH,), F32),
+            pltpu.VMEM((TOK,), jnp.int32),
             pltpu.VMEM((2, 2, 3 * TOK, W), BF),
             pltpu.VMEM((2, TOK, W), BF),
             pltpu.VMEM((TOK, W), BF),
@@ -449,20 +514,21 @@
             pltpu.VMEM((8, 8, TOK), F32),
             pltpu.VMEM((8, 32, W), BF),
             pltpu.VMEM((8, 32, W), BF),
-            dma((200,)),
+            dma((11,)),
+            dma((120,)),
             dma((8,)),
             dma((8,)),
             dma((8,)),
             dma((8,)),
             dma((2, 2, 2)),
-            dma((2, 2, 4, 3)),
+            dma((2, 2, 4)),
             dma((2, 4)),
             dma((2, 4)),
-            dma((2, 2, 4, 3)),
-            dma((2, 10)),
+            dma((2, 2, 4)),
+            dma((2, 9)),
         ],
         compiler_params=pltpu.CompilerParams(
-            collective_id=0, has_side_effects=True, vmem_limit_bytes=40 * 1024 * 1024
+            collective_id=0, has_side_effects=True, vmem_limit_bytes=56 * 1024 * 1024
         ),
     )(
         keyframes,
@@ -470,14 +536,14 @@
         q_high,
         k_high,
         v_high,
-        gain_qh.reshape(1, W),
-        gain_kh.reshape(1, W),
+        gain_qh,
+        gain_kh,
         q_low,
         k_low,
         v_low,
-        gain_ql.reshape(1, WIDTH),
-        gain_kl.reshape(1, WIDTH),
-        permutation.reshape(1, TOK),
+        gain_ql,
+        gain_kl,
+        permutation,
     )
 
 

time: 95.1 us -> 79.7 us (0.84)
  Pallas kernels: 84.8 us -> 77.2 us
  local copies, waits for them, and re-layouts: 9.16 us -> 1.65 us
    pallas_call x1, Pallas kernels: 84.8 us -> 77.2 us  [body(): pl.pallas_call(kernel, out_shape=jax.ShapeDtypeStruct((LOCAL, WIDTH), BF)...]
    unnamed x21 -> x1, local copies, waits for them, and re-layouts: 7.77 us -> 1.65 us
    reshape x2 -> x0, local copies, waits for them, and re-layouts: 1.39 us -> none  [the longest x1 0.7 us: body(): gain_kh.reshape(1, W)]
where the time goes in v2:
time: 79.7 us; the launch traced here: 79.5 us
  Pallas kernels  77.2 us (97%)
  local copies, waits for them, and re-layouts  1.65 us (2%)
    pallas_call x1, Pallas kernels, body(): pl.pallas_call(kernel, out_shape=jax.ShapeDtypeStruct((LOCAL, WIDTH), BF)...  77.2 us
    unnamed x1, local copies, waits for them, and re-layouts  1.65 us

profile of v2, /device:TPU:1, one launch (start us, length us, event | category | flops | bytes accessed | tf_op | source)
XLA Modules:
  0.0 79.5 jit_solution(14836227622223828787)
XLA Ops:
  0.7 77.2 %shard_map.127 = bf16[24,5120]{1,0:T(8,128)(2,1)} custom-call(s32[2]{0:T(128)} %kf.1, s32[1]{0:T(128)S(6)} %copy.15.step_ref, bf16[192,640]{1,0:T(8,128)(2,1)} %q_high_hbm.1, bf16[192,640]{1,0:T(8,128)(2,1)} %k_high_hbm.1, bf16[192,640]{1,0:T(8,128)(2,1)} %v_high_hbm.1, f32[640]{0:T(1024)} %gain_qh_hbm.1, f32[640]{0:T(1024)} %gain_kh_hbm.1, ...), custom_call_target="tpu_custom_call" | custom-call | tf_op jit(solution)/shard_map/pallas_call | solution.py:485
  77.9 1.7 %copy.16 = bf16[24,5120]{1,0:T(8,128)(2,1)} copy(bf16[24,5120]{1,0:T(8,128)(2,1)} %shard_map.127) | data formatting | bytes 491520

commit v3 on v2

v3 whole, which is shorter than its diff:
```python
import functools
import math

import jax
import jax.numpy as jnp
from jax import lax
from jax.experimental import pallas as pl
from jax.experimental.pallas import tpu as pltpu
from jax.sharding import PartitionSpec as P

HEADS = 40
HD = 128
STEPS = 40
EPS = 1e-06
TOK = 192
W = 640
WIDTH = HEADS * HD
LOCAL = 24
BF = jnp.bfloat16
F32 = jnp.float32
MESH = pl.DeviceIdType.MESH
GROUPS = ((0, 2), (2, 4), (4, 5))
QSCALE = HD ** (-0.5) * math.log2(math.e)


def kernel(
    kf_hbm,
    step_hbm,
    q_high_hbm,
    k_high_hbm,
    v_high_hbm,
    gain_qh_hbm,
    gain_kh_hbm,
    q_low_hbm,
    k_low_hbm,
    v_low_hbm,
    gain_ql_hbm,
    gain_kl_hbm,
    perm_hbm,
    out,
    kf,
    step_ref,
    q_high,
    q_low,
    k_low,
    v_low,
    gain_qh,
    gain_kh,
    gain_ql,
    gain_kl,
    perm,
    KV,
    Q,
    OH,
    CH,
    H1R,
    RZ,
    ZC,
    RY,
    SKV,
    RKV,
    SQ,
    RQ,
    SS,
    RS,
    FO,
    FS,
    FC,
    FZ,
    FY,
    FK,
    MB,
    RB,
    load_sems,
    send_sems,
    sum_sems,
    fs_sems,
    fz_sems,
    fy_sems,
    akv_sems,
    aq_sems,
    back_sems,
    h1_sems,
    rz_sems,
    ry_sems,
    yg_sems,
    ag_sems,
    sb_sems,
):
    f = lax.axis_index("frame")
    h = lax.axis_index("head")
    z = f // 8
    y = (f // 2) % 4
    c = f % 2
    sgn = (1 - 2 * c, 2 * c - 1)

    def at(zz, yy, cc, hh):
        return {"frame": (zz * 4 + yy) * 2 + cc, "head": hh}

    def zat(distance):
        return (z + distance + 8) % 8

    sibling = at(z, y, 1 - c, h)
    zdev = [at(zat(s), y, c, h) for s in sgn]
    zdev2 = [at(zat(2 * s), y, c, h) for s in sgn]
    zidx = [zat(j) for j in range(8)]
    zall = [at(zidx[j], y, c, h) for j in range(8)]
    yidx = [(y + j) % 4 for j in range(4)]
    ydev = [at(z, yidx[j], c, h) for j in range(4)]
    hidx = [(h + j) % 8 for j in range(8)]
    hdev = [at(z, y, c, hidx[j]) for j in range(8)]

    barrier = pltpu.get_barrier_semaphore()
    partners = [sibling] + zall[1:] + ydev[1:] + hdev[1:]
    for dev in partners:
        pl.semaphore_signal(barrier, inc=1, device_id=dev, device_id_type=MESH)

    loads = {}
    for name, src, dst in (
        ("kh", k_high_hbm, KV.at[0, 0, pl.ds(0, TOK)]),
        ("vh", v_high_hbm, KV.at[0, 1, pl.ds(0, TOK)]),
        ("kf", kf_hbm, kf),
        ("kl", k_low_hbm, k_low),
        ("vl", v_low_hbm, v_low),
        ("gkl", gain_kl_hbm, gain_kl),
        ("qh", q_high_hbm, q_high),
        ("ql", q_low_hbm, q_low),
        ("gql", gain_ql_hbm, gain_ql),
        ("gkh", gain_kh_hbm, gain_kh),
        ("gqh", gain_qh_hbm, gain_qh),
        ("perm", perm_hbm, perm),
        ("step", step_hbm, step_ref),
    ):
        loads[name] = pltpu.make_async_copy(src, dst, load_sems.at[len(loads)])
        loads[name].start()

    def loaded(*names):
        for name in names:
            loads[name].wait()

    count = [0]
    ends = []

    def rcopy(src, dst, rsem, dev, cond=None):
        index = count[0]
        count[0] += 1
        copy = pltpu.make_async_remote_copy(
            src_ref=src,
            dst_ref=dst,
            send_sem=send_sems.at[index],
            recv_sem=rsem,
            device_id=dev,
            device_id_type=MESH,
        )
        if cond is None:
            copy.start()
        else:
            pl.when(cond)(copy.start)
        ends.append((copy, cond))

    def arrived(dst, rsem, cond=None):
        copy = pltpu.make_async_remote_copy(
            src_ref=dst,
            dst_ref=dst,
            send_sem=send_sems.at[0],
            recv_sem=rsem,
            device_id=sibling,
            device_id_type=MESH,
        )
        if cond is None:
            copy.wait_recv()
        else:
            pl.when(cond)(copy.wait_recv)

    def chunk(k, n=1):
        return pl.ds(16 * k, 16 * n)

    def held(e, o, k, n, core):
        row = TOK + TOK * (o // 4) + 96 * (o % 2) + 48 * core + 16 * k
        return KV.at[e, (o // 2) % 2, pl.ds(pl.multiple_of(row, 16), 16 * n)]

    def place(e, o, k, n=1):
        return held(e, o, k, n, c)

    def root_of(o):
        return jnp.where(o // 4 == 0, kf[0], kf[1])

    def h1_rows(rh, core):
        return pl.ds(pl.multiple_of(96 * rh + 48 * core, 16), 48)

    def h1_send(e):
        for kv in range(2):
            for rh in range(2):
                rcopy(
                    KV.at[e, kv, h1_rows(rh, 1 - c)],
                    H1R.at[e, kv, rh],
                    h1_sems.at[e, kv, rh],
                    sibling,
                )

    def gather_pair(e):
        for kv in range(2):
            for rh in range(2):
                arrived(H1R.at[e, kv, rh], h1_sems.at[e, kv, rh])
                mine = KV[e, kv, h1_rows(rh, c)]
                other = H1R[e, kv, rh]
                for s in range(2):
                    CH[e, s * 4 + kv * 2 + rh] = jnp.where(kf[s] % 2 == c, mine, other)

    far = ((0, 1), (2,))

    def rs_first(e):
        for k in range(3):
            for d in range(2):
                o3, o4 = zat(3 * sgn[d]), zat(4)
                if k in far[d]:
                    rcopy(CH.at[e, o4, chunk(k)], RZ.at[e, d, 1, chunk(k)], rz_sems.at[e, d, 1, k], zdev2[d])
                rcopy(CH.at[e, o3, chunk(k)], RZ.at[e, d, 0, chunk(k)], rz_sems.at[e, d, 0, k], zdev[d])
        for k in range(3):
            for d in range(2):
                o1 = zat(sgn[d])
                rcopy(CH.at[e, o1, chunk(k)], RZ.at[e, d, 2, chunk(k)], rz_sems.at[e, d, 2, k], zdev[d])

    def rs_second(e):
        for k in range(3):
            for d in range(2):
                o2 = zat(2 * sgn[d])
                away = ((z - root_of(o2) // 8) * sgn[d] + 8) % 8
                arrived(RZ.at[e, d, 0, chunk(k)], rz_sems.at[e, d, 0, k])
                value = jnp.where(away == 0, CH[e, o2, chunk(k)], RZ[e, d, 0, chunk(k)])
                if k in far[d]:
                    arrived(RZ.at[e, d, 1, chunk(k)], rz_sems.at[e, d, 1, k])
                    value = jnp.where(away == 2, RZ[e, d, 1, chunk(k)], value)
                RZ[e, d, 0, chunk(k)] = value
                rcopy(RZ.at[e, d, 0, chunk(k)], RZ.at[e, d, 3, chunk(k)], rz_sems.at[e, d, 3, k], zdev2[d])

    def yowner(k):
        return (k + 2 * c) % 4

    def y_send(e):
        away = ((z - root_of(z) // 8) * sgn[0] + 8) % 8
        for k in range(3):
            for d in range(2):
                arrived(RZ.at[e, d, 2, chunk(k)], rz_sems.at[e, d, 2, k])
                arrived(RZ.at[e, d, 3, chunk(k)], rz_sems.at[e, d, 3, k])
            limit = 5 if k in far[0] else 4
            value = jnp.where(away == 1, RZ[e, 0, 2, chunk(k)], RZ[e, 0, 3, chunk(k)])
            value = jnp.where(away >= limit, RZ[e, 1, 3, chunk(k)], value)
            value = jnp.where(away == 7, RZ[e, 1, 2, chunk(k)], value)
            ZC[e, k] = jnp.where(away == 0, CH[e, z, chunk(k)], value)
            yo = yowner(k)
            rcopy(ZC.at[e, k], RY.at[e, y], ry_sems.at[e, y], at(z, yo, c, h), cond=yo != y)

    kown = (y - 2 * c + 4) % 4
    own = kown < 3
    kme = jnp.minimum(kown, 2)
    order = [(kme + j) % 3 for j in range(3)]

    def y_own(e):
        @pl.when(own)
        def _():
            for j in range(1, 4):
                arrived(RY.at[e, yidx[j]], ry_sems.at[e, yidx[j]])
            RY[e, y] = ZC[e, kme]
            root = (root_of(z) // 2) % 4
            value = RY[e, 0]
            for yy in range(1, 4):
                value = jnp.where(root == yy, RY[e, yy], value)
            place(e, z, kme)[...] = value

        piece = place(e, z, kme)
        for j in range(1, 4):
            rcopy(piece, piece, yg_sems.at[e, kme], ydev[j], cond=own)

    def sib_send(e, o, k, i):
        piece = place(e, o, k)
        rcopy(piece, piece, sb_sems.at[e, i, k], sibling)

    def ag_first(e):
        for k in order:
            piece = place(e, z, k)
            arrived(piece, yg_sems.at[e, k], cond=yowner(k) != y)
            for d in range(2):
                rcopy(piece, piece, ag_sems.at[e, d, 1, k], zdev2[d])
            for d in range(2):
                rcopy(piece, piece, ag_sems.at[e, d, 0, k], zdev[d])
            sib_send(e, z, k, 0)

    def ag_second(e):
        for k in order:
            for d in range(2):
                piece = place(e, zat(-2 * sgn[d]), k)
                arrived(piece, ag_sems.at[e, d, 1, k])
                rcopy(piece, piece, ag_sems.at[e, d, 3, k], zdev2[d], cond=k < 2 if d == 0 else k == 2)
                rcopy(piece, piece, ag_sems.at[e, d, 2, k], zdev[d])
                sib_send(e, zat(-2 * sgn[d]), k, 1 + d)
        for k in order:
            for d in range(2):
                arrived(place(e, zat(-sgn[d]), k), ag_sems.at[e, d, 0, k])
                sib_send(e, zat(-sgn[d]), k, 3 + d)

    def ag_last(e):
        for k in order:
            for d in range(2):
                arrived(place(e, zat(-3 * sgn[d]), k), ag_sems.at[e, d, 2, k])
                sib_send(e, zat(-3 * sgn[d]), k, 5 + d)
            piece = place(e, zat(4), k)
            for d in range(2):
                arrived(piece, ag_sems.at[e, d, 3, k], cond=k < 2 if d == 0 else k == 2)
            sib_send(e, zat(4), k, 7)

    def sib_wait(e):
        for k in range(3):
            arrived(held(e, z, k, 1, 1 - c), sb_sems.at[e, 0, k])
            for d in range(2):
                for base, dist in ((1, 2), (3, 1), (5, 3)):
                    arrived(held(e, zat(-dist * sgn[1 - d]), k, 1, 1 - c), sb_sems.at[e, base + d, k])
            arrived(held(e, zat(4), k, 1, 1 - c), sb_sems.at[e, 7, k])

    def rows_sum(values):
        x = values.astype(F32)
        x = x * x
        hi = x.astype(BF)
        lo = (x - hi.astype(F32)).astype(BF)
        ones = jnp.ones((8, W), BF)
        dims = (((1,), (1,)), ((), ()))
        return lax.dot_general(ones, hi, dims, preferred_element_type=F32) + lax.dot_general(
            ones, lo, dims, preferred_element_type=F32
        )

    def factor(ref):
        x = ref[...].astype(F32)
        return lax.rsqrt(jnp.sum(x * x, axis=1, keepdims=True) / WIDTH + EPS)

    def low_keys_pack():
        loaded("kl", "vl", "gkl")
        fk = factor(k_low)
        for p in range(8):
            cols = slice(W * p, W * p + W)
            kn = k_low[:, cols].astype(F32) * fk * gain_kl[cols].reshape(1, W)
            SKV[p] = jnp.concatenate([kn, v_low[:, cols].astype(F32)], axis=0).astype(BF)
        RKV[h] = SKV[h]

    def low_queries_pack():
        loaded("ql", "gql")
        fq = factor(q_low)
        for p in range(8):
            cols = slice(W * p, W * p + W)
            qn = q_low[:, cols].astype(F32) * (fq * QSCALE) * gain_ql[cols].reshape(1, W)
            SQ[p] = jnp.concatenate([qn, jnp.zeros((8, W), F32)], axis=0).astype(BF)
        RQ[h] = SQ[h]

    def low_keys():
        for j in range(1, 8):
            arrived(RKV.at[hidx[j]], akv_sems.at[hidx[j]])
        for p in range(4):
            a = RKV[2 * p].astype(F32)
            b = RKV[2 * p + 1].astype(F32)
            rows = slice(48 * p, 48 * p + 48)
            KV[1, 0, rows] = jnp.concatenate([a[:LOCAL], b[:LOCAL]], axis=0).astype(BF)
            KV[1, 1, rows] = jnp.concatenate([a[LOCAL:], b[LOCAL:]], axis=0).astype(BF)

    def low_queries():
        for j in range(1, 8):
            arrived(RQ.at[hidx[j]], aq_sems.at[hidx[j]])
        for p in range(4):
            a = RQ[2 * p].astype(F32)
            b = RQ[2 * p + 1].astype(F32)
            Q[1, 48 * p : 48 * p + 48] = jnp.concatenate([a[:LOCAL], b[:LOCAL]], axis=0).astype(BF)

    def factors():
        for j in range(1, 8):
            arrived(RS.at[hidx[j]], sum_sems.at[hidx[j]])
        total = RS[0]
        for p in range(1, 8):
            total = total + RS[p]
        FO[...] = lax.rsqrt(total / WIDTH + EPS)
        rcopy(FO, FS, fs_sems.at[0], sibling)

    def factors_z():
        arrived(FS, fs_sems.at[0])
        key = lax.broadcasted_iota(jnp.int32, (8, TOK), 0) - 4
        pick = [jnp.where(kf[s] % 2 == c, FO[...], FS[...]) for s in range(2)]
        FC[...] = jnp.where(key == 0, pick[0], pick[1])
        for j in (4, 3, 5, 2, 6, 1, 7):
            rcopy(FC, FZ.at[z], fz_sems.at[z], zall[j])

    def by_slot(values, roots):
        row = lax.broadcasted_iota(jnp.int32, (8, TOK), 0)
        key = jnp.where(row == 4, roots[0], roots[1])
        total = values[0]
        for i in range(1, len(values)):
            total = jnp.where(key == i, values[i], total)
        return total

    def factors_y():
        FZ[z] = FC[...]
        for j in range(1, 8):
            arrived(FZ.at[zidx[j]], fz_sems.at[zidx[j]])
        FY[y] = by_slot([FZ[i] for i in range(8)], [kf[s] // 8 for s in range(2)])
        for j in range(1, 4):
            rcopy(FY.at[y], FY.at[y], fy_sems.at[y], ydev[j])

    def factors_done():
        for j in range(1, 4):
            arrived(FY.at[yidx[j]], fy_sems.at[yidx[j]])
        FK[...] = by_slot([FY[i] for i in range(4)], [(kf[s] // 2) % 4 for s in range(2)])

    def high_queries():
        loaded("gkh", "gqh", "perm")
        pick = jnp.where(lax.broadcasted_iota(jnp.int32, (8, HD), 0) == 0, QSCALE, 0.0)
        qfac = lax.dot_general(
            FO[...],
            pick,
            (((0,), (0,)), ((), ())),
            precision=lax.Precision.HIGHEST,
            preferred_element_type=F32,
        )
        token = lax.broadcasted_iota(jnp.int32, (TOK, TOK), 0)
        hot = jnp.where(token == perm[...].reshape(1, TOK), 1.0, 0.0).astype(BF)
        for g in range(5):
            cols = slice(HD * g, HD * g + HD)
            gains = (gain_qh[cols] * gain_kh[cols]).reshape(1, HD)
            qn = (q_high[:, cols].astype(F32) * qfac * gains).astype(BF)
            Q[0, :, cols] = lax.dot_general(
                hot, qn, (((0,), (0,)), ((), ())), preferred_element_type=F32
            ).astype(BF)

    def attend(e, cols):
        s = lax.dot_general(
            Q[e, :, cols],
            KV[e, 0, :, cols],
            (((1,), (1,)), ((), ())),
            preferred_element_type=F32,
        )
        if e == 0:
            s = s * jnp.concatenate([FO[4:5], FK[4:5], FK[5:6]], axis=1)
        p = jnp.exp2(s - jnp.max(s, axis=1, keepdims=True)).astype(BF)
        both = jnp.concatenate([KV[e, 1, :, cols], jnp.ones((3 * TOK, HD), BF)], axis=1)
        o = lax.dot_general(p, both, (((1,), (0,)), ((), ())), preferred_element_type=F32)
        return (o[:, :HD] / o[:, HD:]).astype(BF)

    def high_heads():
        def one(g, carry):
            cols = pl.ds(pl.multiple_of(g * HD, HD), HD)
            OH[:, cols] = attend(0, cols)
            return carry

        lax.fori_loop(0, 5, one, 0)

    def low_heads():
        loaded("step")
        lam = step_ref[0].astype(F32) / STEPS
        for i, (start, stop) in enumerate(GROUPS):

            def one(g, carry):
                cols = pl.ds(pl.multiple_of(g * HD, HD), HD)
                mixed = (1.0 - lam) * OH[:, cols].astype(F32) + lam * attend(1, cols).astype(F32)
                pad = jnp.zeros((8, HD), F32)
                for p in range(8):
                    rows = mixed[LOCAL * p : LOCAL * p + LOCAL]
                    MB[p, :, cols] = jnp.concatenate([rows, pad], axis=0).astype(BF)
                return carry

            lax.fori_loop(start, stop, one, 0)
            cols = pl.ds(HD * start, HD * (stop - start))
            for j in range(1, 8):
                rcopy(MB.at[hidx[j], :, cols], RB.at[h, :, cols], back_sems.at[i, h], hdev[j])

    low_keys_pack()
    loaded("kh", "vh", "kf")
    pl.semaphore_wait(barrier, len(partners))
    h1_send(0)
    for j in range(1, 8):
        rcopy(SKV.at[hidx[j]], RKV.at[h], akv_sems.at[h], hdev[j])
    loaded("qh")
    half = lax.broadcasted_iota(jnp.int32, (8, TOK), 0)
    SS[...] = jnp.where(half < 4, rows_sum(q_high[...]), rows_sum(KV[0, 0, 0:TOK]))
    RS[h] = SS[...]
    for j in range(1, 8):
        rcopy(SS, RS.at[h], sum_sems.at[h], hdev[j])
    gather_pair(0)
    rs_first(0)
    low_queries_pack()
    for j in range(1, 8):
        rcopy(SQ.at[hidx[j]], RQ.at[h], aq_sems.at[h], hdev[j])
    factors()
    rs_second(0)
    low_keys()
    h1_send(1)
    factors_z()
    high_queries()
    y_send(0)
    gather_pair(1)
    rs_first(1)
    y_own(0)
    factors_y()
    rs_second(1)
    ag_first(0)
    low_queries()
    y_send(1)
    ag_second(0)
    y_own(1)
    factors_done()
    ag_last(0)
    ag_first(1)
    sib_wait(0)
    ag_second(1)
    high_heads()
    ag_last(1)
    sib_wait(1)
    low_heads()

    RB[h] = MB[h]
    for j in range(1, 8):
        for i, (start, stop) in enumerate(GROUPS):
            cols = pl.ds(HD * start, HD * (stop - start))
            arrived(RB.at[hidx[j], :, cols], back_sems.at[i, hidx[j]])
    for p in range(8):
        out[:, W * p : W * p + W] = RB[p, 0:LOCAL]

    for copy, cond in ends:
        if cond is None:
            copy.wait_send()
        else:
            pl.when(cond)(copy.wait_send)


def body(
    q_high,
    k_high,
    v_high,
    gain_qh,
    gain_kh,
    q_low,
    k_low,
    v_low,
    gain_ql,
    gain_kl,
    keyframes,
    switch_step,
    permutation,
):
    vmem = pl.BlockSpec(memory_space=pltpu.VMEM)
    hbm = pl.BlockSpec(memory_space=pl.ANY)
    dma = pltpu.SemaphoreType.DMA
    return pl.pallas_call(
        kernel,
        out_shape=jax.ShapeDtypeStruct((LOCAL, WIDTH), BF),
        in_specs=[hbm] * 13,
        out_specs=vmem,
        scratch_shapes=[
            pltpu.SMEM((2,), jnp.int32),
            pltpu.SMEM((1,), jnp.int32),
            pltpu.VMEM((TOK, W), BF),
            pltpu.VMEM((LOCAL, WIDTH), BF),
            pltpu.VMEM((LOCAL, WIDTH), BF),
            pltpu.VMEM((LOCAL, WIDTH), BF),
            pltpu.VMEM((W,), F32),
            pltpu.VMEM((W,), F32),
            pltpu.VMEM((WIDTH,), F32),
            pltpu.VMEM((WIDTH,), F32),
            pltpu.VMEM((TOK,), jnp.int32),
            pltpu.VMEM((2, 2, 3 * TOK, W), BF),
            pltpu.VMEM((2, TOK, W), BF),
            pltpu.VMEM((TOK, W), BF),
            pltpu.VMEM((2, 8, 48, W), BF),
            pltpu.VMEM((2, 2, 2, 48, W), BF),
            pltpu.VMEM((2, 2, 4, 48, W), BF),
            pltpu.VMEM((2, 3, 16, W), BF),
            pltpu.VMEM((2, 4, 16, W), BF),
            pltpu.VMEM((8, 48, W), BF),
            pltpu.VMEM((8, 48, W), BF),
            pltpu.VMEM((8, 32, W), BF),
            pltpu.VMEM((8, 32, W), BF),
            pltpu.VMEM((8, TOK), F32),
            pltpu.VMEM((8, 8, TOK), F32),
            pltpu.VMEM((8, TOK), F32),
            pltpu.VMEM((8, TOK), F32),
            pltpu.VMEM((8, TOK), F32),
            pltpu.VMEM((8, 8, TOK), F32),
            pltpu.VMEM((4, 8, TOK), F32),
            pltpu.VMEM((8, TOK), F32),
            pltpu.VMEM((8, 32, W), BF),
            pltpu.VMEM((8, 32, W), BF),
            dma((13,)),
            dma((280,)),
            dma((8,)),
            dma((1,)),
            dma((8,)),
            dma((4,)),
            dma((8,)),
            dma((8,)),
            dma((3, 8)),
            dma((2, 2, 2)),
            dma((2, 2, 4, 3)),
            dma((2, 4)),
            dma((2, 3)),
            dma((2, 2, 4, 3)),
            dma((2, 8, 3)),
        ],
        compiler_params=pltpu.CompilerParams(
            collective_id=0, has_side_effects=True, vmem_limit_bytes=56 * 1024 * 1024
        ),
    )(
        keyframes,
        switch_step,
        q_high,
        k_high,
        v_high,
        gain_qh,
        gain_kh,
        q_low,
        k_low,
        v_low,
        gain_ql,
        gain_kl,
        permutation,
    )


def solution(mesh):
    return jax.shard_map(
        body,
        mesh=mesh,
        in_specs=(
            P("frame", "head"),
            P("frame", "head"),
            P("frame", "head"),
            P("head"),
            P("head"),
            P(("frame", "head"), None),
            P(("frame", "head"), None),
            P(("frame", "head"), None),
            P(),
            P(),
            P(),
            P(),
            P(),
        ),
        out_specs=P(("frame", "head"), None),
        check_vma=False,
    )
```

time: 79.7 us -> 75.1 us (0.942)
  Pallas kernels: 77.2 us -> 72.6 us
    pallas_call x1, Pallas kernels: 77.2 us -> 72.6 us  [body(): pl.pallas_call(kernel, out_shape=jax.ShapeDtypeStruct((LOCAL, WIDTH), BF)...]
where the time goes in v3:
time: 75.1 us; the launch traced here: 74.9 us
  Pallas kernels  72.6 us (97%)
  local copies, waits for them, and re-layouts  1.65 us (2%)
    pallas_call x1, Pallas kernels, body(): pl.pallas_call(kernel, out_shape=jax.ShapeDtypeStruct((LOCAL, WIDTH), BF)...  72.6 us
    unnamed x1, local copies, waits for them, and re-layouts  1.65 us

profile of v3, /device:TPU:1, one launch (start us, length us, event | category | flops | bytes accessed | tf_op | source)
XLA Modules:
  0.0 74.9 jit_solution(7957835869637210764)
XLA Ops:
  0.7 72.6 %shard_map.127 = bf16[24,5120]{1,0:T(8,128)(2,1)} custom-call(s32[2]{0:T(128)} %kf_hbm.1, s32[1]{0:T(128)S(6)} %copy.15.step_hbm, bf16[192,640]{1,0:T(8,128)(2,1)} %q_high_hbm.1, bf16[192,640]{1,0:T(8,128)(2,1)} %k_high_hbm.1, bf16[192,640]{1,0:T(8,128)(2,1)} %v_high_hbm.1, f32[640]{0:T(1024)} %gain_qh_hbm.1, f32[640]{0:T(1024)} %gain_kh_hbm.1, ...), custom_call_target="tpu_custom_call" | custom-call | tf_op jit(solution)/shard_map/pallas_call | solution.py:547
  73.3 1.7 %copy.16 = bf16[24,5120]{1,0:T(8,128)(2,1)} copy(bf16[24,5120]{1,0:T(8,128)(2,1)} %shard_map.127) | data formatting | bytes 491520

commit v4 on v3

--- a/solution.py
+++ b/solution.py
@@ -446,7 +446,7 @@
             OH[:, cols] = attend(0, cols)
             return carry
 
-        lax.fori_loop(0, 5, one, 0)
+        lax.fori_loop(0, 5, one, 0, unroll=True)
 
     def low_heads():
         loaded("step")
@@ -462,7 +462,7 @@
                     MB[p, :, cols] = jnp.concatenate([rows, pad], axis=0).astype(BF)
                 return carry
 
-            lax.fori_loop(start, stop, one, 0)
+            lax.fori_loop(start, stop, one, 0, unroll=True)
             cols = pl.ds(HD * start, HD * (stop - start))
             for j in range(1, 8):
                 rcopy(MB.at[hidx[j], :, cols], RB.at[h, :, cols], back_sems.at[i, h], hdev[j])
@@ -482,35 +482,44 @@
     gather_pair(0)
     rs_first(0)
     low_queries_pack()
-    for j in range(1, 8):
-        rcopy(SQ.at[hidx[j]], RQ.at[h], aq_sems.at[h], hdev[j])
     factors()
     rs_second(0)
     low_keys()
     h1_send(1)
     factors_z()
-    high_queries()
-    y_send(0)
     gather_pair(1)
     rs_first(1)
+    y_send(0)
+    high_queries()
+    rs_second(1)
+    factors_y()
     y_own(0)
-    factors_y()
-    rs_second(1)
+    y_send(1)
     ag_first(0)
+    y_own(1)
+    for j in range(1, 8):
+        rcopy(SQ.at[hidx[j]], RQ.at[h], aq_sems.at[h], hdev[j])
+    ag_second(0)
+    factors_done()
+    ag_first(1)
+    ag_last(0)
+    ag_second(1)
+    sib_wait(0)
     low_queries()
-    y_send(1)
-    ag_second(0)
-    y_own(1)
-    factors_done()
-    ag_last(0)
-    ag_first(1)
-    sib_wait(0)
-    ag_second(1)
     high_heads()
     ag_last(1)
     sib_wait(1)
     low_heads()
 
+    def sent(copies):
+        for copy, cond in copies:
+            if cond is None:
+                copy.wait_send()
+            else:
+                pl.when(cond)(copy.wait_send)
+
+    late = 7 * len(GROUPS)
+    sent(ends[:-late])
     RB[h] = MB[h]
     for j in range(1, 8):
         for i, (start, stop) in enumerate(GROUPS):
@@ -519,11 +528,7 @@
     for p in range(8):
         out[:, W * p : W * p + W] = RB[p, 0:LOCAL]
 
-    for copy, cond in ends:
-        if cond is None:
-            copy.wait_send()
-        else:
-            pl.when(cond)(copy.wait_send)
+    sent(ends[-late:])
 
 
 def body(

time: 75.1 us -> 70.4 us (0.937)
  Pallas kernels: 72.6 us -> 67.9 us
    pallas_call x1, Pallas kernels: 72.6 us -> 67.9 us  [body(): pl.pallas_call(kernel, out_shape=jax.ShapeDtypeStruct((LOCAL, WIDTH), BF)...]
where the time goes in v4:
time: 70.4 us; the launch traced here: 70.2 us
  Pallas kernels  67.9 us (96%)
  local copies, waits for them, and re-layouts  1.65 us (2%)
    pallas_call x1, Pallas kernels, body(): pl.pallas_call(kernel, out_shape=jax.ShapeDtypeStruct((LOCAL, WIDTH), BF)...  67.9 us
    unnamed x1, local copies, waits for them, and re-layouts  1.65 us

profile of v4, /device:TPU:1, one launch (start us, length us, event | category | flops | bytes accessed | tf_op | source)
XLA Modules:
  0.0 70.2 jit_solution(18256108838676724077)
XLA Ops:
  0.7 67.9 %shard_map.127 = bf16[24,5120]{1,0:T(8,128)(2,1)} custom-call(s32[2]{0:T(128)} %kf_hbm.1, s32[1]{0:T(128)S(6)} %copy.15.step_hbm, bf16[192,640]{1,0:T(8,128)(2,1)} %q_high_hbm.1, bf16[192,640]{1,0:T(8,128)(2,1)} %k_high_hbm.1, bf16[192,640]{1,0:T(8,128)(2,1)} %v_high_hbm.1, f32[640]{0:T(1024)} %gain_qh_hbm.1, f32[640]{0:T(1024)} %gain_kh_hbm.1, ...), custom_call_target="tpu_custom_call" | custom-call | tf_op jit(solution)/shard_map/pallas_call | solution.py:552
  68.5 1.7 %copy.16 = bf16[24,5120]{1,0:T(8,128)(2,1)} copy(bf16[24,5120]{1,0:T(8,128)(2,1)} %shard_map.127) | data formatting | bytes 491520

commit v5 on v4

--- a/solution.py
+++ b/solution.py
@@ -107,7 +107,8 @@
     zall = [at(zidx[j], y, c, h) for j in range(8)]
     yidx = [(y + j) % 4 for j in range(4)]
     ydev = [at(z, yidx[j], c, h) for j in range(4)]
-    hidx = [(h + j) % 8 for j in range(8)]
+    hops = ((0, 0), (2, 1), (2, 0), (1, 1), (3, 1), (1, 0), (3, 0), (0, 1))
+    hidx = [((h // 2 + dx) % 4) * 2 + (h + dl) % 2 for dx, dl in hops]
     hdev = [at(z, y, c, hidx[j]) for j in range(8)]
 
     barrier = pltpu.get_barrier_semaphore()
@@ -470,9 +471,9 @@
     low_keys_pack()
     loaded("kh", "vh", "kf")
     pl.semaphore_wait(barrier, len(partners))
-    h1_send(0)
     for j in range(1, 8):
         rcopy(SKV.at[hidx[j]], RKV.at[h], akv_sems.at[h], hdev[j])
+    h1_send(0)
     loaded("qh")
     half = lax.broadcasted_iota(jnp.int32, (8, TOK), 0)
     SS[...] = jnp.where(half < 4, rows_sum(q_high[...]), rows_sum(KV[0, 0, 0:TOK]))
@@ -482,28 +483,28 @@
     gather_pair(0)
     rs_first(0)
     low_queries_pack()
-    factors()
     rs_second(0)
     low_keys()
     h1_send(1)
-    factors_z()
     gather_pair(1)
     rs_first(1)
     y_send(0)
-    high_queries()
     rs_second(1)
-    factors_y()
+    factors()
     y_own(0)
     y_send(1)
+    factors_z()
     ag_first(0)
+    high_queries()
     y_own(1)
     for j in range(1, 8):
         rcopy(SQ.at[hidx[j]], RQ.at[h], aq_sems.at[h], hdev[j])
+    factors_y()
+    ag_first(1)
     ag_second(0)
+    ag_second(1)
     factors_done()
-    ag_first(1)
     ag_last(0)
-    ag_second(1)
     sib_wait(0)
     low_queries()
     high_heads()

time: 70.4 us -> 66.7 us (0.947)
  Pallas kernels: 67.9 us -> 63.8 us
    pallas_call x1, Pallas kernels: 67.9 us -> 63.8 us  [body(): pl.pallas_call(kernel, out_shape=jax.ShapeDtypeStruct((LOCAL, WIDTH), BF)...]
where the time goes in v5:
time: 66.7 us; the launch traced here: 66.1 us
  Pallas kernels  63.8 us (96%)
  local copies, waits for them, and re-layouts  1.65 us (2%)
    pallas_call x1, Pallas kernels, body(): pl.pallas_call(kernel, out_shape=jax.ShapeDtypeStruct((LOCAL, WIDTH), BF)...  63.8 us
    unnamed x1, local copies, waits for them, and re-layouts  1.65 us

profile of v5, /device:TPU:1, one launch (start us, length us, event | category | flops | bytes accessed | tf_op | source)
XLA Modules:
  0.0 66.1 jit_solution(9928600453839116996)
XLA Ops:
  0.7 63.8 %shard_map.127 = bf16[24,5120]{1,0:T(8,128)(2,1)} custom-call(s32[2]{0:T(128)} %kf_hbm.1, s32[1]{0:T(128)S(6)} %copy.15.step_hbm, bf16[192,640]{1,0:T(8,128)(2,1)} %q_high_hbm.1, bf16[192,640]{1,0:T(8,128)(2,1)} %k_high_hbm.1, bf16[192,640]{1,0:T(8,128)(2,1)} %v_high_hbm.1, f32[640]{0:T(1024)} %gain_qh_hbm.1, f32[640]{0:T(1024)} %gain_kh_hbm.1, ...), custom_call_target="tpu_custom_call" | custom-call | tf_op jit(solution)/shard_map/pallas_call | solution.py:553
  64.5 1.7 %copy.16 = bf16[24,5120]{1,0:T(8,128)(2,1)} copy(bf16[24,5120]{1,0:T(8,128)(2,1)} %shard_map.127) | data formatting | bytes 491520
